TPU v7x, 512 devices: a whole 4x8x8 slice. The times are simulated.
512 devices in a mesh: kgrp: 16 (over x_lo, y), ga: 32 (over z, x_hi, core).
Axes of the slice: x: 4 (x_hi: 2, x_lo: 2; x = x_hi * 2 + x_lo), y: 8, z: 8, core: 2. Of those that a mesh axis runs over, the one named last changes fastest.
Arguments:
- pairs: bfloat16 [2, 16, 256, 2, 4096], P(None, 'kgrp', None, None, 'ga'), may hold values from -6 to 6
- screening: bfloat16 [16, 2, 4096, 4096], P('kgrp', None, None, 'ga'), may hold values from -0.09375 to 0.09375
- kq_index: int32 [2, 16], replicated, may hold values from 0 to 15, as said below
- umklapp: int32 [2, 16], replicated, may hold values from 0 to 4095
- occupancy: float32 [16, 2], replicated, may hold values from 0.15 to 1.5
Outputs:
- sigma: float32 [16, 2, 256, 256], P('kgrp', None, 'ga')
Inputs may be any that keep to these rules, and one draw needn't show every extreme that they name: `kq_index`: each round's row is a permutation of the k-point indices.
All inputs are finite; a program needn't handle non-finite values.
Results may differ from a plain program's by a relative error of at most 0.0029.
Values may be sent and summed in bfloat16 or wider, within the bound.
A program may use at most 64 MiB of HBM per device.

v0:
```python
import math

import jax
import jax.numpy as jnp
from jax import lax
from jax.sharding import PartitionSpec as P

ROUNDS = 2


def from_behind(value, axis, steps):
    count = lax.axis_size(axis)
    pairs = [(source, (source + steps) % count) for source in range(count)]
    return lax.ppermute(value, axis, pairs)


def lookups(kq_index, umklapp, occupancy, round_index, owner_group, k_count):
    start_row = owner_group * k_count
    kq_rows = lax.dynamic_slice_in_dim(kq_index[round_index], start_row, k_count)
    shifts = lax.dynamic_slice_in_dim(umklapp[round_index], start_row, k_count)
    compare = kq_rows[:, None] == jnp.arange(occupancy.shape[0], dtype=jnp.int32)[None, :]
    weights = jnp.sum(jnp.where(compare[:, :, None], occupancy[None, :, :], 0.0), axis=1)
    return (shifts, weights)


def partial_sigma(local_pairs, screen_block, shifts, weights):
    gathered = lax.all_gather(local_pairs, "ga", axis=3, tiled=True)
    k_count, band_count, summed_count, column_count = local_pairs.shape
    grid_count = gathered.shape[3]
    column_start = lax.axis_index("ga") * column_count
    aligned = jnp.roll(gathered[0], -shifts[0], axis=2)
    left_rows = aligned.reshape(band_count * summed_count, grid_count)
    projected = jnp.einsum(
        "rg,wgh->wrh", left_rows, screen_block, preferred_element_type=jnp.float32
    )
    projected = projected.reshape(projected.shape[0], band_count, summed_count, column_count)
    scaled = (projected * weights[0][None, None, :, None]).astype(jnp.bfloat16)
    right_cols = lax.dynamic_slice_in_dim(aligned, column_start, column_count, 2)
    results = [jnp.einsum("wbjh,cjh->wbc", scaled, right_cols, preferred_element_type=jnp.float32)]
    return jnp.stack(results, axis=0)


def reduce_rows(partial_value):
    return lax.psum_scatter(partial_value, "ga", scatter_dimension=2, tiled=True)


def per_device(pairs, screening, kq_index, umklapp, occupancy):
    group_index = lax.axis_index("kgrp")
    k_count = pairs.shape[1]
    screen_block = screening[0]
    grid_count = screen_block.shape[1]
    screen_held = screen_block
    sigma_sum = None
    for round_index in range(ROUNDS):
        if round_index > 0:
            screen_held = from_behind(screen_held, "kgrp", 1)
        shifts, weights = lookups(kq_index, umklapp, occupancy, round_index, group_index, k_count)
        partial_value = partial_sigma(pairs[round_index], screen_held, shifts, weights)
        partial_value = reduce_rows(partial_value)
        sigma_sum = partial_value if sigma_sum is None else sigma_sum + partial_value
    return sigma_sum / math.sqrt(grid_count)


def solution(mesh):
    return jax.shard_map(
        per_device,
        mesh=mesh,
        in_specs=(P(None, "kgrp", None, None, "ga"), P("kgrp", None, None, "ga"), P(), P(), P()),
        out_specs=P("kgrp", None, "ga", None),
        check_vma=False,
    )
```

profile of v0, /device:TPU:1, one launch (start us, length us, event | category | flops | bytes accessed | tf_op | source)
XLA Modules:
  0.0 380.9 jit_solution(10036443227697347322)
XLA Ops:
  6.5 1.1 fusion.22
  7.7 0.7 copy.15
  8.4 0.0 all-gather.7.cloned.1.call-update
  8.4 0.0 all-gather.5.cloned.1.call-start
  8.4 0.7 copy.14
  9.1 0.0 all-gather.5.cloned.1.call-update
  9.1 0.0 reduce-scatter.2.cloned.1.call-start
  9.2 4.0 %collective-permute-start = (bf16[2,4096,128]{2,1,0:T(8,128)(2,1)}, bf16[2,4096,128]{2,1,0:T(8,128)(2,1)}, u32[]{:S(2)}, u32[]{:S(2)}) collective-permute-start(bf16[2,4096,128]{2,1,0:T(8,128)(2,1)} %bitcast.42), channel_id=1, source_target_pairs={{0,32},{32,64},{64,96},{96,128},{128,160},{160,192},{192,224},{224... | collective-permute-start | bytes 6291464 | tf_op jit(solution)/shard_map/ppermute | solution.py:14
  13.2 0.8 fusion.23
  14.0 0.7 fusion.25
  18.7 0.8 fusion.24
  19.5 0.7 constant_dynamic-slice_fusion
  20.2 0.6 iota_compare_fusion
  20.8 0.7 iota_compare_fusion.1
  21.5 0.8 select_reduce_fusion.1
  22.4 115.0 %all-gather.7.cloned.1.call-done = bf16[1,1,256,2,4096]{4,2,3,1,0:T(8,128)(2,1)} async-done(((bf16[1,1,256,2,128]{4,2,3,1,0:T(8,128)(2,1)}), bf16[1,1,256,2,4096]{4,2,3,1,0:T(8,128)(2,1)}) %all-gather.7.cloned.1.call-update) | async-done | bytes 4194320 | tf_op jit(solution)/shard_map/all_gather | solution.py:27
  137.4 5.0 %fusion = bf16[256,2,4096]{2,0,1:T(8,128)(2,1)S(1)} fusion(s32[]{:T(128)S(6)} %select_n.38, bf16[256,2,4096]{2,0,1:T(8,128)(2,1)} %bitcast.36), kind=kLoop, calls=%fused_computation.8 | loop fusion | flops 8388608 | bytes 8388612 | tf_op jit(solution)/shard_map/jit(_roll_dynamic)/concatenate | solution.py:31
  142.4 6.3 %copy.10 = bf16[256,2,4096]{2,1,0:T(2,128)(2,1)} copy(bf16[256,2,4096]{2,0,1:T(8,128)(2,1)S(1)} %fusion) | data formatting | bytes 8388608 | tf_op jit(solution)/shard_map/jit(_roll_dynamic)/dynamic_slice | solution.py:31
  148.7 7.2 %reshape.62 = bf16[512,4096,1]{1,0,2:T(8,128)(2,1)} reshape(bf16[256,2,4096]{2,1,0:T(2,128)(2,1)} %copy.10) | data formatting | bytes 8388608 | tf_op jit(solution)/shard_map/reshape | solution.py:32
  155.9 74.4 %all-gather.5.cloned.1.call-done = bf16[1,1,256,2,4096]{4,2,3,1,0:T(8,128)(2,1)} async-done(((bf16[1,1,256,2,128]{4,2,3,1,0:T(8,128)(2,1)}), bf16[1,1,256,2,4096]{4,2,3,1,0:T(8,128)(2,1)}) %all-gather.5.cloned.1.call-update) | async-done | bytes 4194320 | tf_op jit(solution)/shard_map/all_gather | solution.py:27
  230.4 5.3 %fusion.1 = bf16[256,2,4096]{2,0,1:T(8,128)(2,1)S(1)} fusion(s32[]{:T(128)S(6)} %select_n.36, bf16[256,2,4096]{2,0,1:T(8,128)(2,1)} %bitcast.38), kind=kLoop, calls=%fused_computation.9 | loop fusion | flops 8388608 | bytes 8388612 | tf_op jit(solution)/shard_map/jit(_roll_dynamic)/concatenate | solution.py:31
  235.7 6.3 %copy.7 = bf16[256,2,4096]{2,1,0:T(2,128)(2,1)} copy(bf16[256,2,4096]{2,0,1:T(8,128)(2,1)S(1)} %fusion.1) | data formatting | bytes 8388608 | tf_op jit(solution)/shard_map/jit(_roll_dynamic)/dynamic_slice | solution.py:31
  242.0 7.4 %reshape.59 = bf16[512,4096,1]{1,0,2:T(8,128)(2,1)} reshape(bf16[256,2,4096]{2,1,0:T(2,128)(2,1)} %copy.7) | data formatting | bytes 8388608 | tf_op jit(solution)/shard_map/reshape | solution.py:32
  249.4 3.6 fusion.20
  253.0 0.0 collective-permute-done
  253.0 3.0 fusion.27
  256.0 0.4 convolution_bitcast_fusion
  256.5 1.7 copy-done.1
  258.2 1.2 fusion.3
  259.4 0.0 reduce-scatter.2.cloned.1.call-update
  259.4 113.6 %reduce-scatter.2.cloned.1.call-done = f32[1,2,8,256]{3,2,1,0:T(8,128)} async-done(((f32[1,2,256,256]{3,2,1,0:T(8,128)}), f32[1,2,8,256]{3,2,1,0:T(8,128)}) %reduce-scatter.2.cloned.1.call-update) | async-done | bytes 16400 | tf_op jit(solution)/shard_map/reduce_scatter | solution.py:44
  373.1 1.3 broadcast_multiply_fusion
  (8 shorter events, 0.0 us)
Async XLA Ops:
  6.5 130.9 %all-gather.7.cloned.1.call-start = ((), (), s32[]{:S(2)}) async-start(), calls=%async_computation.2 | async-start | bytes 4325376 | tf_op jit(solution)/shard_map/all_gather | solution.py:27
  8.4 222.0 %all-gather.5.cloned.1.call-start = ((), (), s32[]{:S(2)}) async-start(), calls=%async_computation.1 | async-start | bytes 4325376 | tf_op jit(solution)/shard_map/all_gather | solution.py:27
  9.1 363.9 %reduce-scatter.2.cloned.1.call-start = ((), (), s32[]{:S(2)}) async-start(), calls=%async_computation.3 | async-start | bytes 540672 | tf_op jit(solution)/shard_map/reduce_scatter | solution.py:44
  9.2 243.8 %collective-permute-start = (bf16[2,4096,128]{2,1,0:T(8,128)(2,1)}, bf16[2,4096,128]{2,1,0:T(8,128)(2,1)}, u32[]{:S(2)}, u32[]{:S(2)}) collective-permute-start(bf16[2,4096,128]{2,1,0:T(8,128)(2,1)} %bitcast.42), channel_id=1, source_target_pairs={{0,32},{32,64},{64,96},{96,128},{128,160},{160,192},{192,224},{224... | collective-permute-start | bytes 6291464 | tf_op jit(solution)/shard_map/ppermute | solution.py:14
  242.0 7.4 %copy-start.3 = (bf16[1,2,4096,128]{3,2,1,0:T(8,128)(2,1)S(1)}, bf16[1,2,4096,128]{3,2,1,0:T(8,128)(2,1)}, u32[]{:S(2)}) copy-start(bf16[1,2,4096,128]{3,2,1,0:T(8,128)(2,1)} %param.8) | copy-start | bytes 6291460
  249.4 3.6 copy-start.2
  253.0 3.1 copy-start
  256.0 2.2 copy-start.1
Sparse Core Ops, SparseCore 0:
  10.5 126.8 all-gather.6
  140.5 89.7 all-gather.4
  259.6 113.4 reduce-scatter.1
where the time goes:
time: 386 us; the launch traced here: 381 us
  waiting for transfers between devices  303 us (78%)
  local copies, waits for them, and re-layouts  33.6 us (9%)
  between operations  17.3 us (4%)
  other arithmetic  14.5 us (4%)
  matrix products  8.22 us (2%)
  starting transfers between devices  4.12 us (1%)
    all_gather x2, waiting for transfers between devices, partial_sigma(): gathered = lax.all_gather(local_pairs, 'ga', axis=3, tiled=True)  189 us
    reduce_scatter x1, waiting for transfers between devices, reduce_rows(): lax.psum_scatter(partial_value, 'ga', scatter_dimension=2, tiled=True)  114 us
    reshape x2, local copies, waits for them, and re-layouts, partial_sigma(): left_rows = aligned.reshape(band_count * summed_count, grid_count)  14.6 us
    dynamic_slice x2, local copies, waits for them, and re-layouts, partial_sigma(): aligned = jnp.roll(gathered[0], -shifts[0], axis=2)  12.7 us
    concatenate x2, other arithmetic, partial_sigma(): aligned = jnp.roll(gathered[0], -shifts[0], axis=2)  10.3 us
  transfers between devices with their start and end apart: 4, of which 3 were waited for; matrix products, arithmetic and copies ran while one was open for 12% of the time, Pallas kernels for 0%

commit v1 on v0

v1 whole, which is shorter than its diff:
```python
import functools
import math

import jax
import jax.numpy as jnp
from jax import lax
from jax.experimental import pallas as pl
from jax.experimental.pallas import tpu as pltpu
from jax.sharding import PartitionSpec as P

ROUNDS = 2
GROUPS = 16
RING = 8
SIDES = 2
CORES = 2
LANES = 128
PARTS = 2
MESH = pl.DeviceIdType.MESH

Z0 = 0
X0 = Z0 + 2 * 4 * PARTS
Y1 = X0 + RING * PARTS
Z1 = Y1 + SIDES * PARTS
C = Z1 + SIDES * 2 * 4 * PARTS
S = C + ROUNDS * SIDES * RING
A = S + ROUNDS * 2
COUNT = A + ROUNDS * RING * SIDES


def kernel(
    pairs,
    screening,
    kq_index,
    umklapp,
    occupancy,
    out,
    all0,
    all1,
    screen,
    shift_rows,
    total,
    right,
    partial,
    sibling_part,
    outgoing,
    incoming,
    send,
    recv,
    local,
):
    group = lax.axis_index("kgrp")
    place = lax.axis_index("ga")
    z = lax.div(place, 4)
    side = lax.rem(lax.div(place, 2), 2)
    core = lax.rem(place, 2)
    tiles = screening.shape[1]
    grid_count = tiles * LANES
    rows = pairs.shape[1]
    piece = rows // PARTS
    gathered = (all0, all1)

    def at(z_at, side_at, core_at):
        return z_at * 4 + side_at * 2 + core_at

    def along(steps):
        return lax.rem(z + steps + 2 * RING, RING)

    before = lax.rem(group + GROUPS - 1, GROUPS)
    after = lax.rem(group + 1, GROUPS)
    upward = (group, at(along(1), side, core))
    downward = (group, at(along(-1), side, core))
    across = (group, at(z, 1 - side, core))
    sibling = (group, at(z, side, 1 - core))

    def copy(source, target, index, device):
        return pltpu.make_async_remote_copy(
            src_ref=source,
            dst_ref=target,
            send_sem=send.at[index],
            recv_sem=recv.at[index],
            device_id=device,
            device_id_type=MESH,
        )

    def cut(part):
        return pl.ds(part * piece, piece)

    def z_of(k):
        steps = lax.div(k + 1, 2)
        return along(jnp.where(lax.rem(k, 2) == 1, -steps, steps))

    def k_of(step, way):
        return 2 * step - 1 + way if step < 4 else 7

    def origin(step, way):
        return along(-step if way == 0 else step)

    def ring_copy(rnd, cross, way, step, part):
        came_from = origin(step - 1, way)
        place_of = at(came_from, lax.rem(side + cross, 2), core)
        target = gathered[rnd].at[place_of, cut(part)]
        source = pairs.at[0, cut(part)] if rnd == 0 and step == 1 else target
        index = (Z0 if rnd == 0 else Z1) + ((cross * 2 + way) * 4 + step - 1) * PARTS + part
        return copy(source, target, index, upward if way == 0 else downward)

    def ring_arrival(rnd, cross, way, step, part):
        place_of = at(origin(step, way), lax.rem(side + cross, 2), core)
        target = gathered[rnd].at[place_of, cut(part)]
        index = (Z0 if rnd == 0 else Z1) + ((cross * 2 + way) * 4 + step - 1) * PARTS + part
        return copy(target, target, index, upward)

    def cross_copy(k, part, own=False):
        target = all0.at[at(z_of(k), side, core), cut(part)]
        source = pairs.at[0, cut(part)] if own else target
        return copy(source, target, X0 + k * PARTS + part, across)

    def cross_arrival(k, part):
        target = all0.at[at(z_of(k), 1 - side, core), cut(part)]
        return copy(target, target, X0 + k * PARTS + part, across)

    def group_copy(cross, part):
        target = all1.at[place, cut(part)]
        device = (before, at(z, lax.rem(side + cross, 2), core))
        return copy(pairs.at[1, cut(part)], target, Y1 + cross * PARTS + part, device)

    def group_arrival(cross, part):
        target = all1.at[at(z, lax.rem(side + cross, 2), core), cut(part)]
        return copy(target, target, Y1 + cross * PARTS + part, sibling)

    def core_copy(rnd, cross, k, own=False):
        target = gathered[rnd].at[at(z_of(k), lax.rem(side + cross, 2), core)]
        source = pairs.at[0] if own else target
        return copy(source, target, C + (rnd * 2 + cross) * RING + k, sibling)

    def core_arrival(rnd, cross, k):
        target = gathered[rnd].at[at(z_of(k), lax.rem(side + cross, 2), 1 - core)]
        return copy(target, target, C + (rnd * 2 + cross) * RING + k, sibling)

    def sum_copy(rnd, w):
        return copy(partial.at[rnd, w, :, 1 - core], sibling_part.at[rnd, w], S + rnd * 2 + w, sibling)

    def spread_copy(rnd, i):
        z_to = lax.rem(z + lax.div(i, 2), RING)
        side_to = lax.rem(side + lax.rem(i, 2), 2)
        device = (group if rnd == 0 else after, at(z_to, side_to, core))
        index = A + rnd * RING * SIDES + i
        return copy(outgoing.at[rnd, z_to * 2 + side_to], incoming.at[rnd, i], index, device)

    barrier = pltpu.get_barrier_semaphore()
    for device in (
        upward,
        downward,
        across,
        sibling,
        (after, place),
        (after, at(z, 1 - side, core)),
    ):
        pl.semaphore_signal(barrier, inc=1, device_id=device, device_id_type=MESH)
    whole = pltpu.make_async_copy(screening, screen.at[:, pl.ds(0, tiles)], local.at[0])
    whole.start()
    wrap = pltpu.make_async_copy(screening.at[:, pl.ds(0, 2)], screen.at[:, pl.ds(tiles, 2)], local.at[1])
    wrap.start()
    mine = pltpu.make_async_copy(pairs.at[0], all0.at[place], local.at[2])
    mine.start()
    pl.semaphore_wait(barrier, 6)

    for part in range(PARTS):
        ring_copy(0, 0, 0, 1, part).start()
        ring_copy(0, 0, 1, 1, part).start()
        cross_copy(0, part, own=True).start()
    for part in range(PARTS):
        for cross in range(SIDES):
            group_copy(cross, part).start()
    core_copy(0, 0, 0, own=True).start()

    k_point = (group, after)
    shift = [umklapp[rnd, k_point[rnd]] for rnd in range(ROUNDS)]
    total[...] = jnp.zeros_like(total)
    for rnd in range(ROUNDS):
        column = lax.broadcasted_iota(jnp.int32, (2 * LANES, 3 * LANES), 1)
        row = lax.broadcasted_iota(jnp.int32, (2 * LANES, 3 * LANES), 0)
        hit = column == row + lax.rem(grid_count - shift[rnd], LANES)
        shift_rows[rnd] = jnp.where(hit, 1.0, 0.0).astype(jnp.bfloat16)
    whole.wait()
    wrap.wait()
    mine.wait()

    def multiply(rnd, cross, first, last):
        def one(k, carry):
            core_arrival(rnd, cross, k).wait_recv()
            chip = z_of(k) * 2 + lax.rem(side + cross, 2)
            start = lax.rem(chip * 2 * LANES + grid_count - shift[rnd], grid_count)
            tile = lax.div(start, LANES)
            met = jnp.concatenate(
                [jnp.concatenate([screen[w, tile + i] for i in range(3)], axis=0) for w in range(2)], axis=1
            )
            met = jnp.dot(shift_rows[rnd], met, preferred_element_type=jnp.float32)
            left = jnp.concatenate([gathered[rnd][chip * 2], gathered[rnd][chip * 2 + 1]], axis=1)
            product = jnp.dot(left, met.astype(jnp.bfloat16), preferred_element_type=jnp.float32)
            for w in range(2):
                total[rnd, w] += product[:, w * LANES : (w + 1) * LANES]
            return carry

        lax.fori_loop(first, last, one, 0)

    def take_across(first, last):
        for k in range(first, last):
            for part in range(PARTS):
                cross_arrival(k, part).wait_recv()
            core_copy(0, 1, k).start()

    def contract(rnd):
        begin = lax.rem(place + lax.div(shift[rnd], LANES), 2 * RING * SIDES)
        follow = lax.rem(begin + 1, 2 * RING * SIDES)
        row = lax.broadcasted_iota(jnp.int32, (2 * LANES, LANES), 0)
        column = lax.broadcasted_iota(jnp.int32, (2 * LANES, LANES), 1)
        hit = row == column + lax.rem(shift[rnd], LANES)
        pick = jnp.where(hit, 1.0, 0.0).astype(jnp.bfloat16)
        near = jnp.concatenate([gathered[rnd][begin], gathered[rnd][follow]], axis=1)
        right[...] = jnp.dot(near, pick, preferred_element_type=jnp.float32)
        bands = rows // 2
        others = jnp.concatenate(
            [right[pl.ds(j, bands, stride=2), :].astype(jnp.bfloat16) for j in range(2)], axis=1
        )
        weight = [occupancy[kq_index[rnd, k_point[rnd]], j] for j in range(2)]
        for w in range(2):
            scaled = [total[rnd, w, pl.ds(j, bands, stride=2), :] * weight[j] for j in range(2)]
            left = jnp.concatenate(scaled, axis=1).astype(jnp.bfloat16)
            sums = lax.dot_general(
                left, others, (((1,), (1,)), ((), ())), preferred_element_type=jnp.float32
            )
            partial[rnd, w] = sums.reshape(partial.shape[2:])
            sum_copy(rnd, w).start()

    def spread(rnd):
        added = []
        for w in range(2):
            sum_copy(rnd, w).wait_recv()
            added.append(partial[rnd, w, :, core] + sibling_part[rnd, w])
        outgoing[rnd] = jnp.concatenate(added, axis=1).astype(jnp.bfloat16)

        def one(i, carry):
            spread_copy(rnd, i).start()
            return carry

        lax.fori_loop(1 - rnd, RING * SIDES, one, 0)

    for step in range(1, 4):
        for part in range(PARTS):
            for way in range(2):
                ring_arrival(0, 0, way, step, part).wait_recv()
                if step < 3 or part * 2 // PARTS == way:
                    ring_copy(0, 0, way, step + 1, part).start()
                cross_copy(k_of(step, way), part).start()
        for way in range(2):
            core_copy(0, 0, k_of(step, way)).start()
        multiply(0, 0, max(0, 2 * step - 3), 2 * step - 1)

    for cross in range(SIDES):
        for part in range(PARTS):
            group_arrival(cross, part).wait_recv()
            for way in range(2):
                ring_copy(1, cross, way, 1, part).start()
        core_copy(1, cross, 0).start()
    for part in range(PARTS):
        ring_arrival(0, 0, part * 2 // PARTS, 4, part).wait_recv()
        cross_copy(7, part).start()
    core_copy(0, 0, 7).start()
    multiply(0, 0, 5, 7)

    between = {
        (1, 0): lambda: (take_across(0, 3), multiply(0, 0, 7, 8)),
        (1, 1): lambda: (take_across(3, 4), multiply(0, 1, 0, 2)),
        (1, 2): lambda: multiply(0, 1, 2, 4),
        (1, 3): lambda: (take_across(4, 5), multiply(1, 0, 0, 1)),
        (2, 0): lambda: (take_across(5, 6), multiply(0, 1, 4, 5), multiply(1, 1, 0, 1)),
        (2, 1): lambda: multiply(1, 0, 1, 3),
        (2, 2): lambda: (take_across(6, 7), multiply(1, 1, 1, 3)),
        (2, 3): lambda: multiply(0, 1, 5, 6),
        (3, 0): lambda: multiply(0, 1, 6, 7),
        (3, 1): lambda: multiply(1, 0, 3, 5),
        (3, 2): lambda: (take_across(7, 8), multiply(1, 1, 3, 5)),
        (3, 3): lambda: (multiply(0, 1, 7, 8), contract(0)),
        (4, 0): lambda: (spread(0), multiply(1, 0, 5, 7)),
        (4, 1): lambda: multiply(1, 1, 5, 7),
    }
    for step in range(1, 5):
        for cross in range(SIDES):
            for part in range(PARTS):
                for way in range(2):
                    if step == 4 and part * 2 // PARTS != way:
                        continue
                    ring_arrival(1, cross, way, step, part).wait_recv()
                    if step < 3 or (step == 3 and part * 2 // PARTS == way):
                        ring_copy(1, cross, way, step + 1, part).start()
                if step < 4:
                    if part == PARTS - 1:
                        for way in range(2):
                            core_copy(1, cross, k_of(step, way)).start()
                    between[(step, cross * 2 + part * 2 // PARTS)]()
            if step == 4:
                core_copy(1, cross, 7).start()
                between[(step, cross)]()
    multiply(1, 0, 7, 8)
    multiply(1, 1, 7, 8)
    contract(1)
    spread(1)

    def settle(i, carry):
        spread_copy(0, i).wait_recv()
        return carry

    lax.fori_loop(1, RING * SIDES, settle, 0)
    chip = z * 2 + side
    own = jnp.concatenate([partial[0, w, chip, core] + sibling_part[0, w, chip] for w in range(2)], axis=0)
    result = own + jnp.sum(incoming[0, 1:].astype(jnp.float32), axis=0)
    for step in range(1, 5):
        for part in range(PARTS):
            for way in range(2):
                if step == 4 and part * 2 // PARTS != way:
                    continue
                ring_copy(0, 0, way, step, part).wait_send()
                for cross in range(SIDES):
                    ring_copy(1, cross, way, step, part).wait_send()
    for part in range(PARTS):
        for cross in range(SIDES):
            group_copy(cross, part).wait_send()
        for k in range(RING):
            cross_copy(k, part, own=k == 0).wait_send()
    for rnd in range(ROUNDS):
        for cross in range(SIDES):
            for k in range(RING):
                core_copy(rnd, cross, k).wait_send()
        for w in range(2):
            sum_copy(rnd, w).wait_send()

    def sent(i, carry):
        spread_copy(0, i).wait_send()
        return carry

    lax.fori_loop(1, RING * SIDES, sent, 0)

    def last(i, carry):
        spread_copy(1, i).wait()
        return carry

    lax.fori_loop(0, RING * SIDES, last, 0)
    result = result + jnp.sum(incoming[1].astype(jnp.float32), axis=0)
    bands = out.shape[1]
    for w in range(2):
        out[w] = result[w * bands : (w + 1) * bands] * (1.0 / math.sqrt(grid_count))


def per_device(pairs, screening, kq_index, umklapp, occupancy):
    rounds, k_count, band_count, summed_count, column_count = pairs.shape
    rows = band_count * summed_count
    grid_count = screening.shape[2]
    devices = grid_count // column_count
    bands = band_count // devices
    chips = RING * SIDES
    sigma = pl.pallas_call(
        kernel,
        out_shape=jax.ShapeDtypeStruct((2, bands, band_count), jnp.float32),
        in_specs=[
            pl.BlockSpec(memory_space=pl.ANY),
            pl.BlockSpec(memory_space=pl.ANY),
            pl.BlockSpec(memory_space=pltpu.SMEM),
            pl.BlockSpec(memory_space=pltpu.SMEM),
            pl.BlockSpec(memory_space=pltpu.SMEM),
        ],
        out_specs=pl.BlockSpec(memory_space=pltpu.VMEM),
        scratch_shapes=[
            pltpu.VMEM((devices, rows, column_count), jnp.bfloat16),
            pltpu.VMEM((devices, rows, column_count), jnp.bfloat16),
            pltpu.VMEM((2, devices + 2, LANES, column_count), jnp.bfloat16),
            pltpu.VMEM((ROUNDS, 2 * LANES, 3 * LANES), jnp.bfloat16),
            pltpu.VMEM((ROUNDS, 2, rows, column_count), jnp.float32),
            pltpu.VMEM((rows, column_count), jnp.float32),
            pltpu.VMEM((ROUNDS, 2, chips, 2, bands, band_count), jnp.float32),
            pltpu.VMEM((ROUNDS, 2, chips, bands, band_count), jnp.float32),
            pltpu.VMEM((ROUNDS, chips, 2 * bands, band_count), jnp.bfloat16),
            pltpu.VMEM((ROUNDS, chips, 2 * bands, band_count), jnp.bfloat16),
            pltpu.SemaphoreType.DMA((COUNT,)),
            pltpu.SemaphoreType.DMA((COUNT,)),
            pltpu.SemaphoreType.DMA((3,)),
        ],
        compiler_params=pltpu.CompilerParams(
            collective_id=0, has_side_effects=True, vmem_limit_bytes=40 << 20
        ),
    )(
        pairs.reshape(rounds, rows, column_count),
        screening.reshape(2, devices, LANES, column_count),
        kq_index,
        umklapp,
        occupancy,
    )
    return sigma[None]


def solution(mesh):
    return jax.shard_map(
        per_device,
        mesh=mesh,
        in_specs=(P(None, "kgrp", None, None, "ga"), P("kgrp", None, None, "ga"), P(), P(), P()),
        out_specs=P("kgrp", None, "ga", None),
        check_vma=False,
    )
```

time: 386 us -> 71.5 us (0.19); the launches traced: 381 us -> 71.3 us
  waiting for transfers between devices: 303 us -> 0 us
  Pallas kernels: 0 us -> 66 us
  local copies, waits for them, and re-layouts: 33.6 us -> 5.26 us
  between operations: 17.3 us -> 0.01 us
  other arithmetic: 14.5 us -> 0 us
  matrix products: 8.22 us -> 0 us
  starting transfers between devices: 4.12 us -> 0 us
    all_gather x2 -> x0, waiting for transfers between devices: 189 us -> none  [partial_sigma(): gathered = lax.all_gather(local_pairs, 'ga', axis=3, tiled=True)]
    reduce_scatter x1 -> x0, waiting for transfers between devices: 114 us -> none  [reduce_rows(): lax.psum_scatter(partial_value, 'ga', scatter_dimension=2, tiled=True)]
    pallas_call x0 -> x1, Pallas kernels: none -> 66 us  [per_device(): pl.pallas_call(kernel, out_shape=jax.ShapeDtypeStruct((2, bands, band_cou...]
    reshape x2 -> x0, local copies, waits for them, and re-layouts: 14.6 us -> none  [partial_sigma(): left_rows = aligned.reshape(band_count * summed_count, grid_count)]
    dynamic_slice x3 -> x0, local copies, waits for them, and re-layouts: 13.3 us -> none  [the longest x2 12.7 us: partial_sigma(): aligned = jnp.roll(gathered[0], -shifts[0], axis=2)]
    concatenate x2 -> x0, other arithmetic: 10.3 us -> none  [partial_sigma(): aligned = jnp.roll(gathered[0], -shifts[0], axis=2)]
    dot_general x4 -> x0, matrix products: 8.22 us -> none  [the longest x2 6.6 us: partial_sigma(): jnp.einsum('rg,wgh->wrh', left_rows, screen_block, preferred_element_type...]
    ppermute x1 -> x0, starting transfers between devices: 4.04 us -> none  [from_behind(): return lax.ppermute(value, axis, pairs)]
  transfers between devices with their start and end apart: 4 -> 0, of which waited for: 3 -> 0; matrix products, arithmetic and copies ran while one was open for 12% -> 0% of each run, Pallas kernels for 0% -> 0%
where the time goes in v1:
time: 71.5 us; the launch traced here: 71.3 us
  Pallas kernels  66 us (92%)
  local copies, waits for them, and re-layouts  5.26 us (7%)
    pallas_call x1, Pallas kernels, per_device(): pl.pallas_call(kernel, out_shape=jax.ShapeDtypeStruct((2, bands, band_cou...  66 us
    unnamed x10, local copies, waits for them, and re-layouts  5.26 us

profile of v1, /device:TPU:1, one launch (start us, length us, event | category | flops | bytes accessed | tf_op | source)
XLA Modules:
  0.0 71.3 jit_solution(11102732522774166047)
XLA Ops:
  0.0 0.8 %copy.6.occupancy = f32[16,2]{1,0:T(8,128)S(1)} copy(f32[16,2]{0,1:T(2,128)} %param.9) | data formatting | bytes 256 | tf_op args[4]
  0.8 0.0 copy-start
  0.8 1.6 %copy-done = bf16[1,2,4096,128]{3,2,1,0:T(8,128)(2,1)S(1)} copy-done((bf16[1,2,4096,128]{3,2,1,0:T(8,128)(2,1)S(1)}, bf16[1,2,4096,128]{3,2,1,0:T(8,128)(2,1)}, u32[]{:S(2)}) %copy-start) | copy-done | bytes 2097176
  2.3 0.0 copy-start.1
  2.3 0.9 %copy-done.1 = bf16[2,1,256,2,128]{4,3,2,1,0:T(2,128)(2,1)S(1)} copy-done((bf16[2,1,256,2,128]{4,3,2,1,0:T(2,128)(2,1)S(1)}, bf16[2,1,256,2,128]{4,3,2,1,0:T(2,128)(2,1)}, u32[]{:S(2)}) %copy-start.1) | copy-done | bytes 262168
  3.3 0.0 copy-start.2
  3.3 0.7 copy-done.2
  4.0 0.0 copy-start.3
  4.0 0.7 copy-done.3
  4.7 66.0 %shard_map.55 = f32[2,8,256]{2,1,0:T(8,128)S(1)} custom-call(bf16[2,512,128]{2,1,0:T(8,128)(2,1)S(1)} %bitcast.4, bf16[2,32,128,128]{3,2,1,0:T(8,128)(2,1)S(1)} %bitcast.3, s32[2,16]{1,0:T(2,128)S(1)} %copy-done.2, s32[2,16]{1,0:T(2,128)S(1)} %copy-done.3, f32[16,2]{1,0:T(8,128)S(1)} %copy.6.occupancy), custom_call_target="tpu_custom_call" | custom-call | tf_op jit(solution)/shard_map/pallas_call | solution.py:361
  70.7 0.6 copy.8
Async XLA Ops:
  0.8 1.6 %copy-start = (bf16[1,2,4096,128]{3,2,1,0:T(8,128)(2,1)S(1)}, bf16[1,2,4096,128]{3,2,1,0:T(8,128)(2,1)}, u32[]{:S(2)}) copy-start(bf16[1,2,4096,128]{3,2,1,0:T(8,128)(2,1)} %param.6) | copy-start | bytes 6291460
  2.3 0.9 %copy-start.1 = (bf16[2,1,256,2,128]{4,3,2,1,0:T(2,128)(2,1)S(1)}, bf16[2,1,256,2,128]{4,3,2,1,0:T(2,128)(2,1)}, u32[]{:S(2)}) copy-start(bf16[2,1,256,2,128]{4,3,2,1,0:T(2,128)(2,1)} %param.5) | copy-start | bytes 786436
  3.3 0.7 copy-start.2
  4.0 0.7 copy-start.3

commit v2 on v1

--- a/solution.py
+++ b/solution.py
@@ -19,10 +19,11 @@
 
 Z0 = 0
 X0 = Z0 + 2 * 4 * PARTS
-Y1 = X0 + RING * PARTS
+X1 = X0 + RING * PARTS
+Y1 = X1 + PARTS
 Z1 = Y1 + SIDES * PARTS
 C = Z1 + SIDES * 2 * 4 * PARTS
-S = C + ROUNDS * SIDES * RING
+S = C + ROUNDS * SIDES * RING * PARTS
 A = S + ROUNDS * 2
 COUNT = A + ROUNDS * RING * SIDES
 
@@ -30,9 +31,9 @@
 def kernel(
     pairs,
     screening,
-    kq_index,
-    umklapp,
-    occupancy,
+    kq_index_all,
+    umklapp_all,
+    occupancy_all,
     out,
     all0,
     all1,
@@ -44,6 +45,10 @@
     sibling_part,
     outgoing,
     incoming,
+    last_rows,
+    kq_index,
+    umklapp,
+    occupancy,
     send,
     recv,
     local,
@@ -109,14 +114,14 @@
         index = (Z0 if rnd == 0 else Z1) + ((cross * 2 + way) * 4 + step - 1) * PARTS + part
         return copy(target, target, index, upward)
 
-    def cross_copy(k, part, own=False):
-        target = all0.at[at(z_of(k), side, core), cut(part)]
+    def cross_copy(rnd, k, part, own=False):
+        target = gathered[rnd].at[at(z_of(k), side, core), cut(part)]
         source = pairs.at[0, cut(part)] if own else target
-        return copy(source, target, X0 + k * PARTS + part, across)
-
-    def cross_arrival(k, part):
-        target = all0.at[at(z_of(k), 1 - side, core), cut(part)]
-        return copy(target, target, X0 + k * PARTS + part, across)
+        return copy(source, target, (X0 + k * PARTS if rnd == 0 else X1) + part, across)
+
+    def cross_arrival(rnd, k, part):
+        target = gathered[rnd].at[at(z_of(k), 1 - side, core), cut(part)]
+        return copy(target, target, (X0 + k * PARTS if rnd == 0 else X1) + part, across)
 
     def group_copy(cross, part):
         target = all1.at[place, cut(part)]
@@ -127,14 +132,14 @@
         target = all1.at[at(z, lax.rem(side + cross, 2), core), cut(part)]
         return copy(target, target, Y1 + cross * PARTS + part, sibling)
 
-    def core_copy(rnd, cross, k, own=False):
-        target = gathered[rnd].at[at(z_of(k), lax.rem(side + cross, 2), core)]
-        source = pairs.at[0] if own else target
-        return copy(source, target, C + (rnd * 2 + cross) * RING + k, sibling)
-
-    def core_arrival(rnd, cross, k):
-        target = gathered[rnd].at[at(z_of(k), lax.rem(side + cross, 2), 1 - core)]
-        return copy(target, target, C + (rnd * 2 + cross) * RING + k, sibling)
+    def core_copy(rnd, cross, k, part, own=False):
+        target = gathered[rnd].at[at(z_of(k), lax.rem(side + cross, 2), core), cut(part)]
+        source = pairs.at[0, cut(part)] if own else target
+        return copy(source, target, C + ((rnd * 2 + cross) * RING + k) * PARTS + part, sibling)
+
+    def core_arrival(rnd, cross, k, part):
+        target = gathered[rnd].at[at(z_of(k), lax.rem(side + cross, 2), 1 - core), cut(part)]
+        return copy(target, target, C + ((rnd * 2 + cross) * RING + k) * PARTS + part, sibling)
 
     def sum_copy(rnd, w):
         return copy(partial.at[rnd, w, :, 1 - core], sibling_part.at[rnd, w], S + rnd * 2 + w, sibling)
@@ -162,16 +167,26 @@
     wrap.start()
     mine = pltpu.make_async_copy(pairs.at[0], all0.at[place], local.at[2])
     mine.start()
+    tables = [
+        pltpu.make_async_copy(source, target, local.at[3 + i])
+        for i, (source, target) in enumerate(
+            ((kq_index_all, kq_index), (umklapp_all, umklapp), (occupancy_all, occupancy))
+        )
+    ]
+    for table in tables:
+        table.start()
     pl.semaphore_wait(barrier, 6)
 
     for part in range(PARTS):
         ring_copy(0, 0, 0, 1, part).start()
         ring_copy(0, 0, 1, 1, part).start()
-        cross_copy(0, part, own=True).start()
+        cross_copy(0, 0, part, own=True).start()
+        group_copy(0, part).start()
     for part in range(PARTS):
-        for cross in range(SIDES):
-            group_copy(cross, part).start()
-    core_copy(0, 0, 0, own=True).start()
+        group_copy(1, part).start()
+        core_copy(0, 0, 0, part, own=True).start()
+    for table in tables:
+        table.wait()
 
     k_point = (group, after)
     shift = [umklapp[rnd, k_point[rnd]] for rnd in range(ROUNDS)]
@@ -185,29 +200,57 @@
     wrap.wait()
     mine.wait()
 
-    def multiply(rnd, cross, first, last):
-        def one(k, carry):
-            core_arrival(rnd, cross, k).wait_recv()
+    def met_rows(rnd, cross, k):
+        chip = z_of(k) * 2 + lax.rem(side + cross, 2)
+        start = lax.rem(chip * 2 * LANES + grid_count - shift[rnd], grid_count)
+        tile = lax.div(start, LANES)
+        near = jnp.concatenate(
+            [jnp.concatenate([screen[w, tile + i] for i in range(3)], axis=0) for w in range(2)], axis=1
+        )
+        near = jnp.dot(shift_rows[rnd], near, preferred_element_type=jnp.float32)
+        return near.astype(jnp.bfloat16)
+
+    def multiply(rnd, *blocks, met=None):
+        left = []
+        for cross, k in blocks:
+            for part in range(PARTS):
+                core_arrival(rnd, cross, k, part).wait_recv()
             chip = z_of(k) * 2 + lax.rem(side + cross, 2)
-            start = lax.rem(chip * 2 * LANES + grid_count - shift[rnd], grid_count)
-            tile = lax.div(start, LANES)
-            met = jnp.concatenate(
-                [jnp.concatenate([screen[w, tile + i] for i in range(3)], axis=0) for w in range(2)], axis=1
-            )
-            met = jnp.dot(shift_rows[rnd], met, preferred_element_type=jnp.float32)
-            left = jnp.concatenate([gathered[rnd][chip * 2], gathered[rnd][chip * 2 + 1]], axis=1)
-            product = jnp.dot(left, met.astype(jnp.bfloat16), preferred_element_type=jnp.float32)
-            for w in range(2):
-                total[rnd, w] += product[:, w * LANES : (w + 1) * LANES]
-            return carry
-
-        lax.fori_loop(first, last, one, 0)
-
-    def take_across(first, last):
-        for k in range(first, last):
-            for part in range(PARTS):
-                cross_arrival(k, part).wait_recv()
-            core_copy(0, 1, k).start()
+            left += [gathered[rnd][chip * 2], gathered[rnd][chip * 2 + 1]]
+        if met is None:
+            met = jnp.concatenate([met_rows(rnd, cross, k) for cross, k in blocks], axis=0)
+        product = jnp.dot(jnp.concatenate(left, axis=1), met, preferred_element_type=jnp.float32)
+        for w in range(2):
+            total[rnd, w] += product[:, w * LANES : (w + 1) * LANES]
+
+    def take_across(rnd, k):
+        for part in range(PARTS):
+            cross_arrival(rnd, k, part).wait_recv()
+            core_copy(rnd, 1, k, part).start()
+
+    def take_group(cross):
+        for part in range(PARTS):
+            group_arrival(cross, part).wait_recv()
+            for way in range(2):
+                ring_copy(1, cross, way, 1, part).start()
+            core_copy(1, cross, 0, part).start()
+
+    def last_step(rnd, cross):
+        return 3 if rnd == 1 and cross == 1 else 4
+
+    def ways(step, part):
+        return (part,) if step == 4 else (0, 1)
+
+    def take_ring(rnd, cross, step):
+        for part in range(PARTS):
+            for way in ways(step, part):
+                ring_arrival(rnd, cross, way, step, part).wait_recv()
+                if step < last_step(rnd, cross) and way in ways(step + 1, part):
+                    ring_copy(rnd, cross, way, step + 1, part).start()
+                k = k_of(step, way)
+                if rnd == 0 or (cross == 0 and step == 4):
+                    cross_copy(rnd, k, part).start()
+                core_copy(rnd, cross, k, part).start()
 
     def contract(rnd):
         begin = lax.rem(place + lax.div(shift[rnd], LANES), 2 * RING * SIDES)
@@ -222,7 +265,7 @@
         others = jnp.concatenate(
             [right[pl.ds(j, bands, stride=2), :].astype(jnp.bfloat16) for j in range(2)], axis=1
         )
-        weight = [occupancy[kq_index[rnd, k_point[rnd]], j] for j in range(2)]
+        weight = [occupancy[j, kq_index[rnd, k_point[rnd]]] for j in range(2)]
         for w in range(2):
             scaled = [total[rnd, w, pl.ds(j, bands, stride=2), :] * weight[j] for j in range(2)]
             left = jnp.concatenate(scaled, axis=1).astype(jnp.bfloat16)
@@ -245,64 +288,44 @@
 
         lax.fori_loop(1 - rnd, RING * SIDES, one, 0)
 
-    for step in range(1, 4):
-        for part in range(PARTS):
-            for way in range(2):
-                ring_arrival(0, 0, way, step, part).wait_recv()
-                if step < 3 or part * 2 // PARTS == way:
-                    ring_copy(0, 0, way, step + 1, part).start()
-                cross_copy(k_of(step, way), part).start()
-        for way in range(2):
-            core_copy(0, 0, k_of(step, way)).start()
-        multiply(0, 0, max(0, 2 * step - 3), 2 * step - 1)
-
-    for cross in range(SIDES):
-        for part in range(PARTS):
-            group_arrival(cross, part).wait_recv()
-            for way in range(2):
-                ring_copy(1, cross, way, 1, part).start()
-        core_copy(1, cross, 0).start()
-    for part in range(PARTS):
-        ring_arrival(0, 0, part * 2 // PARTS, 4, part).wait_recv()
-        cross_copy(7, part).start()
-    core_copy(0, 0, 7).start()
-    multiply(0, 0, 5, 7)
-
-    between = {
-        (1, 0): lambda: (take_across(0, 3), multiply(0, 0, 7, 8)),
-        (1, 1): lambda: (take_across(3, 4), multiply(0, 1, 0, 2)),
-        (1, 2): lambda: multiply(0, 1, 2, 4),
-        (1, 3): lambda: (take_across(4, 5), multiply(1, 0, 0, 1)),
-        (2, 0): lambda: (take_across(5, 6), multiply(0, 1, 4, 5), multiply(1, 1, 0, 1)),
-        (2, 1): lambda: multiply(1, 0, 1, 3),
-        (2, 2): lambda: (take_across(6, 7), multiply(1, 1, 1, 3)),
-        (2, 3): lambda: multiply(0, 1, 5, 6),
-        (3, 0): lambda: multiply(0, 1, 6, 7),
-        (3, 1): lambda: multiply(1, 0, 3, 5),
-        (3, 2): lambda: (take_across(7, 8), multiply(1, 1, 3, 5)),
-        (3, 3): lambda: (multiply(0, 1, 7, 8), contract(0)),
-        (4, 0): lambda: (spread(0), multiply(1, 0, 5, 7)),
-        (4, 1): lambda: multiply(1, 1, 5, 7),
-    }
-    for step in range(1, 5):
-        for cross in range(SIDES):
-            for part in range(PARTS):
-                for way in range(2):
-                    if step == 4 and part * 2 // PARTS != way:
-                        continue
-                    ring_arrival(1, cross, way, step, part).wait_recv()
-                    if step < 3 or (step == 3 and part * 2 // PARTS == way):
-                        ring_copy(1, cross, way, step + 1, part).start()
-                if step < 4:
-                    if part == PARTS - 1:
-                        for way in range(2):
-                            core_copy(1, cross, k_of(step, way)).start()
-                    between[(step, cross * 2 + part * 2 // PARTS)]()
-            if step == 4:
-                core_copy(1, cross, 7).start()
-                between[(step, cross)]()
-    multiply(1, 0, 7, 8)
-    multiply(1, 1, 7, 8)
+    take_ring(0, 0, 1)
+    take_group(0)
+    multiply(0, (0, 0), (0, 1), (0, 2))
+    take_ring(0, 0, 2)
+    take_group(1)
+    take_across(0, 0)
+    multiply(0, (0, 3), (0, 4), (1, 0))
+    take_ring(1, 0, 1)
+    multiply(1, (0, 0), (1, 0), (0, 1), (0, 2))
+    take_ring(0, 0, 3)
+    take_across(0, 1)
+    multiply(0, (0, 5), (0, 6), (1, 1))
+    take_ring(1, 0, 2)
+    take_across(0, 2)
+    multiply(1, (0, 3), (0, 4))
+    take_ring(1, 1, 1)
+    take_across(0, 3)
+    multiply(0, (1, 2), (1, 3))
+    multiply(1, (1, 1), (1, 2))
+    take_ring(1, 0, 3)
+    take_across(0, 4)
+    multiply(1, (0, 5), (0, 6))
+    take_ring(0, 0, 4)
+    take_ring(1, 0, 4)
+    take_across(0, 5)
+    multiply(0, (0, 7), (1, 4), (1, 5))
+    take_ring(1, 1, 2)
+    take_across(0, 6)
+    multiply(1, (0, 7), (1, 3), (1, 4))
+    for i, k in enumerate((5, 6, 7)):
+        last_rows[i] = met_rows(1, 1, k)
+    take_across(0, 7)
+    multiply(0, (1, 6), (1, 7))
+    contract(0)
+    take_ring(1, 1, 3)
+    spread(0)
+    take_across(1, 7)
+    multiply(1, (1, 5), (1, 6), (1, 7), met=jnp.concatenate([last_rows[i] for i in range(3)], axis=0))
     contract(1)
     spread(1)
 
@@ -314,23 +337,22 @@
     chip = z * 2 + side
     own = jnp.concatenate([partial[0, w, chip, core] + sibling_part[0, w, chip] for w in range(2)], axis=0)
     result = own + jnp.sum(incoming[0, 1:].astype(jnp.float32), axis=0)
-    for step in range(1, 5):
-        for part in range(PARTS):
-            for way in range(2):
-                if step == 4 and part * 2 // PARTS != way:
-                    continue
-                ring_copy(0, 0, way, step, part).wait_send()
-                for cross in range(SIDES):
-                    ring_copy(1, cross, way, step, part).wait_send()
+    for rnd, cross in ((0, 0), (1, 0), (1, 1)):
+        for step in range(1, last_step(rnd, cross) + 1):
+            for part in range(PARTS):
+                for way in ways(step, part):
+                    ring_copy(rnd, cross, way, step, part).wait_send()
     for part in range(PARTS):
         for cross in range(SIDES):
             group_copy(cross, part).wait_send()
         for k in range(RING):
-            cross_copy(k, part, own=k == 0).wait_send()
+            cross_copy(0, k, part, own=k == 0).wait_send()
+        cross_copy(1, 7, part).wait_send()
     for rnd in range(ROUNDS):
         for cross in range(SIDES):
             for k in range(RING):
-                core_copy(rnd, cross, k).wait_send()
+                for part in range(PARTS):
+                    core_copy(rnd, cross, k, part).wait_send()
         for w in range(2):
             sum_copy(rnd, w).wait_send()
 
@@ -364,9 +386,9 @@
         in_specs=[
             pl.BlockSpec(memory_space=pl.ANY),
             pl.BlockSpec(memory_space=pl.ANY),
-            pl.BlockSpec(memory_space=pltpu.SMEM),
-            pl.BlockSpec(memory_space=pltpu.SMEM),
-            pl.BlockSpec(memory_space=pltpu.SMEM),
+            pl.BlockSpec(memory_space=pl.ANY),
+            pl.BlockSpec(memory_space=pl.ANY),
+            pl.BlockSpec(memory_space=pl.ANY),
         ],
         out_specs=pl.BlockSpec(memory_space=pltpu.VMEM),
         scratch_shapes=[
@@ -380,19 +402,23 @@
             pltpu.VMEM((ROUNDS, 2, chips, bands, band_count), jnp.float32),
             pltpu.VMEM((ROUNDS, chips, 2 * bands, band_count), jnp.bfloat16),
             pltpu.VMEM((ROUNDS, chips, 2 * bands, band_count), jnp.bfloat16),
+            pltpu.VMEM((3, 2 * LANES, 2 * column_count), jnp.bfloat16),
+            pltpu.SMEM(kq_index.shape, jnp.int32),
+            pltpu.SMEM(umklapp.shape, jnp.int32),
+            pltpu.SMEM(occupancy.shape[::-1], jnp.float32),
             pltpu.SemaphoreType.DMA((COUNT,)),
             pltpu.SemaphoreType.DMA((COUNT,)),
-            pltpu.SemaphoreType.DMA((3,)),
+            pltpu.SemaphoreType.DMA((6,)),
         ],
         compiler_params=pltpu.CompilerParams(
-            collective_id=0, has_side_effects=True, vmem_limit_bytes=40 << 20
+            collective_id=0, has_side_effects=True, vmem_limit_bytes=62 << 20
         ),
     )(
         pairs.reshape(rounds, rows, column_count),
         screening.reshape(2, devices, LANES, column_count),
         kq_index,
         umklapp,
-        occupancy,
+        occupancy.T,
     )
     return sigma[None]
 

time: 71.5 us -> 65 us (0.909)
  local copies, waits for them, and re-layouts: 5.26 us -> 1.32 us
  Pallas kernels: 66 us -> 63.4 us
    unnamed x10 -> x1, local copies, waits for them, and re-layouts: 5.26 us -> 1.32 us
    pallas_call x1, Pallas kernels: 66 us -> 63.4 us  [per_device(): pl.pallas_call(kernel, out_shape=jax.ShapeDtypeStruct((2, bands, band_cou...]
where the time goes in v2:
time: 65 us; the launch traced here: 64.7 us
  Pallas kernels  63.4 us (98%)
  local copies, waits for them, and re-layouts  1.32 us (2%)
    pallas_call x1, Pallas kernels, per_device(): pl.pallas_call(kernel, out_shape=jax.ShapeDtypeStruct((2, bands, band_cou...  63.4 us
    unnamed x1, local copies, waits for them, and re-layouts  1.32 us

profile of v2, /device:TPU:1, one launch (start us, length us, event | category | flops | bytes accessed | tf_op | source)
XLA Modules:
  0.0 64.7 jit_solution(14149967260032124025)
XLA Ops:
  0.0 63.4 %shard_map.55 = f32[2,8,256]{2,1,0:T(8,128)} custom-call(bf16[2,512,128]{2,1,0:T(8,128)(2,1)} %bitcast.5, bf16[2,32,128,128]{3,2,1,0:T(8,128)(2,1)} %bitcast.4, s32[2,16]{1,0:T(2,128)} %kq_index_all.1, s32[2,16]{1,0:T(2,128)} %umklapp_all.1, f32[2,16]{1,0:T(2,128)} %bitcast.7), custom_call_target="tpu_custom_call" | custom-call | tf_op jit(solution)/shard_map/pallas_call | solution.py:383
  63.4 1.3 %copy.7 = f32[1,2,8,256]{3,2,1,0:T(8,128)} copy(f32[1,2,8,256]{3,2,1,0:T(8,128)} %bitcast.6) | data formatting | bytes 32768

commit v3 on v2

v3 whole, which is shorter than its diff:
```python
import functools
import math

import jax
import jax.numpy as jnp
from jax import lax
from jax.experimental import pallas as pl
from jax.experimental.pallas import tpu as pltpu
from jax.sharding import PartitionSpec as P

ROUNDS = 2
GROUPS = 16
RING = 8
SIDES = 2
CORES = 2
LANES = 128
PARTS = 2
MESH = pl.DeviceIdType.MESH

Z0 = 0
X0 = Z0 + 2 * 4 * PARTS
X1 = X0 + RING * PARTS
Y1 = X1 + 2 * PARTS
Z1 = Y1 + PARTS
C = Z1 + SIDES * 2 * 4 * PARTS
R = C + 2
S = R + ROUNDS
A = S + ROUNDS * 2
COUNT = A + ROUNDS * RING * SIDES


def kernel(
    pairs,
    screening,
    kq_index_all,
    umklapp_all,
    occupancy_all,
    out,
    all0,
    all1,
    screen,
    shift_rows,
    total,
    right,
    right_mine,
    right_theirs,
    partial,
    sibling_part,
    outgoing,
    incoming,
    last_rows,
    kq_index,
    umklapp,
    occupancy,
    send,
    recv,
    local,
):
    group = lax.axis_index("kgrp")
    place = lax.axis_index("ga")
    z = lax.div(place, 4)
    side = lax.rem(lax.div(place, 2), 2)
    core = lax.rem(place, 2)
    tiles = screening.shape[1]
    grid_count = tiles * LANES
    rows = pairs.shape[1]
    piece = rows // PARTS
    gathered = (all0, all1)

    def at(z_at, side_at, core_at):
        return z_at * 4 + side_at * 2 + core_at

    def chip_at(z_at, side_at):
        return z_at * 2 + side_at

    def along(steps):
        return lax.rem(z + steps + 2 * RING, RING)

    before = lax.rem(group + GROUPS - 1, GROUPS)
    after = lax.rem(group + 1, GROUPS)
    upward = (group, at(along(1), side, core))
    downward = (group, at(along(-1), side, core))
    across = (group, at(z, 1 - side, core))
    sibling = (group, at(z, side, 1 - core))

    def copy(source, target, index, device):
        return pltpu.make_async_remote_copy(
            src_ref=source,
            dst_ref=target,
            send_sem=send.at[index],
            recv_sem=recv.at[index],
            device_id=device,
            device_id_type=MESH,
        )

    def cut(part):
        return pl.ds(part * piece, piece)

    def z_of(k):
        steps = lax.div(k + 1, 2)
        return along(jnp.where(lax.rem(k, 2) == 1, -steps, steps))

    def k_of(step, way):
        return 2 * step - 1 + way if step < 4 else 7

    def origin(step, way):
        return along(-step if way == 0 else step)

    def ring_copy(rnd, cross, way, step, part):
        came_from = origin(step - 1, way)
        place_of = chip_at(came_from, lax.rem(side + cross, 2))
        target = gathered[rnd].at[place_of, cut(part)]
        source = pairs.at[0, cut(part)] if rnd == 0 and step == 1 else target
        index = (Z0 if rnd == 0 else Z1) + ((cross * 2 + way) * 4 + step - 1) * PARTS + part
        return copy(source, target, index, upward if way == 0 else downward)

    def ring_arrival(rnd, cross, way, step, part):
        place_of = chip_at(origin(step, way), lax.rem(side + cross, 2))
        target = gathered[rnd].at[place_of, cut(part)]
        index = (Z0 if rnd == 0 else Z1) + ((cross * 2 + way) * 4 + step - 1) * PARTS + part
        return copy(target, target, index, upward)

    def cross_copy(rnd, k, part, own=False):
        target = gathered[rnd].at[chip_at(z_of(k), side), cut(part)]
        source = pairs.at[0, cut(part)] if own else target
        return copy(source, target, (X0 + k * PARTS if rnd == 0 else X1 + (k // 7) * PARTS) + part, across)

    def cross_arrival(rnd, k, part):
        target = gathered[rnd].at[chip_at(z_of(k), 1 - side), cut(part)]
        return copy(target, target, (X0 + k * PARTS if rnd == 0 else X1 + (k // 7) * PARTS) + part, across)

    def group_copy(part):
        target = all1.at[chip_at(z, side), cut(part)]
        return copy(pairs.at[1, cut(part)], target, Y1 + part, (before, place))

    def group_arrival(part):
        target = all1.at[chip_at(z, side), cut(part)]
        return copy(target, target, Y1 + part, sibling)

    def screen_copy(wrap):
        first, count = (tiles, 1) if wrap else (0, tiles)
        target = screen.at[core, :, pl.ds(first, count)]
        return copy(screening.at[:, pl.ds(0, count)], target, C + wrap, sibling)

    def screen_arrival(wrap):
        first, count = (tiles, 1) if wrap else (0, tiles)
        target = screen.at[1 - core, :, pl.ds(first, count)]
        return copy(target, target, C + wrap, sibling)

    def right_copy(rnd):
        return copy(right_mine.at[rnd], right_theirs.at[rnd], R + rnd, sibling)

    def sum_copy(rnd, w):
        return copy(partial.at[rnd, w, :, 1 - core], sibling_part.at[rnd, w], S + rnd * 2 + w, sibling)

    def spread_copy(rnd, i):
        turn = lax.div(i, 2)
        steps = jnp.where(lax.rem(turn, 2) == 1, 4 - lax.div(turn + 1, 2), 4 + lax.div(turn, 2))
        z_to = along(steps)
        side_to = lax.rem(side + 1 - lax.rem(i, 2), 2)
        device = (group if rnd == 0 else after, at(z_to, side_to, core))
        index = A + rnd * RING * SIDES + i
        return copy(outgoing.at[rnd, z_to * 2 + side_to], incoming.at[rnd, i], index, device)

    barrier = pltpu.get_barrier_semaphore()
    for device in (
        upward,
        downward,
        across,
        sibling,
        (after, place),
        (before, place),
    ):
        pl.semaphore_signal(barrier, inc=1, device_id=device, device_id_type=MESH)
    whole = pltpu.make_async_copy(screening, screen.at[core, :, pl.ds(0, tiles)], local.at[0])
    whole.start()
    wrap = pltpu.make_async_copy(screening.at[:, pl.ds(0, 1)], screen.at[core, :, pl.ds(tiles, 1)], local.at[1])
    wrap.start()
    mine = pltpu.make_async_copy(pairs.at[0], all0.at[chip_at(z, side)], local.at[2])
    mine.start()
    tables = [
        pltpu.make_async_copy(source, target, local.at[3 + i])
        for i, (source, target) in enumerate(
            ((kq_index_all, kq_index), (umklapp_all, umklapp), (occupancy_all, occupancy))
        )
    ]
    for table in tables:
        table.start()
    pl.semaphore_wait(barrier, 6)

    for part in range(PARTS):
        ring_copy(0, 0, 0, 1, part).start()
        ring_copy(0, 0, 1, 1, part).start()
        cross_copy(0, 0, part, own=True).start()
        group_copy(part).start()
    for again in range(2):
        screen_copy(again).start()
    for table in tables:
        table.wait()

    k_point = (group, after)
    shift = [umklapp[rnd, k_point[rnd]] for rnd in range(ROUNDS)]
    total[...] = jnp.zeros_like(total)
    for rnd in range(ROUNDS):
        column = lax.broadcasted_iota(jnp.int32, (LANES, 2 * LANES), 1)
        row = lax.broadcasted_iota(jnp.int32, (LANES, 2 * LANES), 0)
        hit = column == row + lax.rem(grid_count - shift[rnd], LANES)
        shift_rows[rnd] = jnp.where(hit, 1.0, 0.0).astype(jnp.bfloat16)

    def met_rows(rnd, cross, k):
        block = chip_at(z_of(k), lax.rem(side + cross, 2)) * 2 + core
        start = lax.rem(block * LANES + grid_count - shift[rnd], grid_count)
        tile = lax.div(start, LANES)
        near = jnp.concatenate(
            [
                jnp.concatenate([screen[c, w, tile + i] for i in range(2)], axis=0)
                for w in range(2)
                for c in range(CORES)
            ],
            axis=1,
        )
        near = jnp.dot(shift_rows[rnd], near, preferred_element_type=jnp.float32)
        return near.astype(jnp.bfloat16)

    def multiply(rnd, *blocks, met=None):
        left = [gathered[rnd][chip_at(z_of(k), lax.rem(side + cross, 2))] for cross, k in blocks]
        if met is None:
            met = jnp.concatenate([met_rows(rnd, cross, k) for cross, k in blocks], axis=0)
        product = jnp.dot(jnp.concatenate(left, axis=1), met, preferred_element_type=jnp.float32)
        for i in range(2 * CORES):
            total[rnd, i] += product[:, i * LANES : (i + 1) * LANES]

    def take_across(rnd, k):
        for part in range(PARTS):
            cross_arrival(rnd, k, part).wait_recv()

    def take_group():
        for part in range(PARTS):
            group_arrival(part).wait_recv()
            for way in range(2):
                ring_copy(1, 0, way, 1, part).start()
            cross_copy(1, 0, part).start()

    def take_group_across():
        for part in range(PARTS):
            cross_arrival(1, 0, part).wait_recv()
            for way in range(2):
                ring_copy(1, 1, way, 1, part).start()

    def last_step(rnd, cross):
        return 3 if rnd == 1 and cross == 1 else 4

    def ways(step, part):
        return (part,) if step == 4 else (0, 1)

    def take_ring(rnd, cross, step, hand_across=True):
        for part in range(PARTS):
            for way in ways(step, part):
                ring_arrival(rnd, cross, way, step, part).wait_recv()
                if step < last_step(rnd, cross) and way in ways(step + 1, part):
                    ring_copy(rnd, cross, way, step + 1, part).start()
                k = k_of(step, way)
                if hand_across and (rnd == 0 or (cross == 0 and step == 4)):
                    cross_copy(rnd, k, part).start()

    def swap_right(rnd):
        for c in range(CORES):
            begin = lax.rem(chip_at(z, side) * 2 + c + lax.div(shift[rnd], LANES), 2 * RING * SIDES)
            late = jnp.where(lax.rem(begin, 2) == core, 0, 1)
            block = lax.rem(begin + late, 2 * RING * SIDES)
            row = lax.broadcasted_iota(jnp.int32, (LANES, LANES), 0) + late * LANES
            column = lax.broadcasted_iota(jnp.int32, (LANES, LANES), 1)
            hit = row == column + lax.rem(shift[rnd], LANES)
            pick = jnp.where(hit, 1.0, 0.0).astype(jnp.bfloat16)
            near = gathered[rnd][lax.div(block, 2)]
            part = jnp.dot(near, pick, preferred_element_type=jnp.float32)
            right_mine[rnd, c] = part.astype(jnp.bfloat16)
        right_copy(rnd).start()

    def contract(rnd):
        bands = rows // 2
        right_copy(rnd).wait_recv()
        for c in range(CORES):
            both = right_mine[rnd, c].astype(jnp.float32) + right_theirs[rnd, c].astype(jnp.float32)
            right[c] = both
        pairs_of = [(j, c) for j in range(2) for c in range(CORES)]
        others = jnp.concatenate(
            [right[c, pl.ds(j, bands, stride=2), :].astype(jnp.bfloat16) for j, c in pairs_of], axis=1
        )
        weight = [occupancy[j, kq_index[rnd, k_point[rnd]]] for j in range(2)]
        for w in range(2):
            scaled = jnp.concatenate(
                [total[rnd, w * CORES + c, pl.ds(j, bands, stride=2), :] * weight[j] for j, c in pairs_of],
                axis=1,
            )
            high = scaled.astype(jnp.bfloat16)
            low = (scaled - high.astype(jnp.float32)).astype(jnp.bfloat16)
            sums = sum(
                lax.dot_general(left, others, (((1,), (1,)), ((), ())), preferred_element_type=jnp.float32)
                for left in (high, low)
            )
            partial[rnd, w] = sums.reshape(partial.shape[2:])
            sum_copy(rnd, w).start()

    def spread(rnd):
        added = []
        for w in range(2):
            sum_copy(rnd, w).wait_recv()
            added.append(partial[rnd, w, :, core] + sibling_part[rnd, w])
        outgoing[rnd] = jnp.concatenate(added, axis=1).astype(jnp.bfloat16)

        def one(i, carry):
            spread_copy(rnd, i).start()
            return carry

        lax.fori_loop(0, RING * SIDES - 1 + rnd, one, 0)

    take_ring(0, 0, 1, hand_across=False)
    take_group()
    for part in range(PARTS):
        for k in (1, 2):
            cross_copy(0, k, part).start()
    take_ring(0, 0, 2)
    whole.wait()
    wrap.wait()
    mine.wait()
    for again in range(2):
        screen_arrival(again).wait_recv()
    multiply(0, (0, 0), (0, 1), (0, 2))
    take_across(0, 0)
    multiply(0, (0, 3), (0, 4), (1, 0))
    take_ring(1, 0, 1)
    take_group_across()
    multiply(1, (0, 0), (1, 0), (0, 1), (0, 2))
    take_ring(0, 0, 3)
    take_across(0, 1)
    multiply(0, (0, 5), (0, 6), (1, 1))
    take_ring(1, 0, 2)
    take_across(0, 2)
    multiply(1, (0, 3), (0, 4))
    take_ring(1, 1, 1)
    take_across(0, 3)
    multiply(0, (1, 2), (1, 3))
    multiply(1, (1, 1), (1, 2))
    take_ring(1, 0, 3)
    take_across(0, 4)
    multiply(1, (0, 5), (0, 6))
    take_ring(0, 0, 4)
    take_ring(1, 0, 4)
    take_across(0, 5)
    multiply(0, (0, 7), (1, 4), (1, 5))
    take_ring(1, 1, 2)
    take_across(0, 6)
    multiply(1, (0, 7), (1, 3), (1, 4))
    take_across(0, 7)
    multiply(0, (1, 6), (1, 7))
    swap_right(0)
    for i, k in enumerate((5, 6, 7)):
        last_rows[i] = met_rows(1, 1, k)
    contract(0)
    take_ring(1, 1, 3)
    spread(0)
    take_across(1, 7)
    swap_right(1)
    multiply(1, (1, 5), (1, 6), (1, 7), met=jnp.concatenate([last_rows[i] for i in range(3)], axis=0))
    contract(1)
    spread(1)

    def settle(i, carry):
        spread_copy(0, i).wait_recv()
        return carry

    lax.fori_loop(0, RING * SIDES - 1, settle, 0)
    chip = z * 2 + side
    own = jnp.concatenate([partial[0, w, chip, core] + sibling_part[0, w, chip] for w in range(2)], axis=0)
    result = own + jnp.sum(incoming[0, : RING * SIDES - 1].astype(jnp.float32), axis=0)
    for again in range(2):
        screen_copy(again).wait_send()
    for rnd, cross in ((0, 0), (1, 0), (1, 1)):
        for step in range(1, last_step(rnd, cross) + 1):
            for part in range(PARTS):
                for way in ways(step, part):
                    ring_copy(rnd, cross, way, step, part).wait_send()
    for part in range(PARTS):
        group_copy(part).wait_send()
        for k in range(RING):
            cross_copy(0, k, part, own=k == 0).wait_send()
        for k in (0, 7):
            cross_copy(1, k, part).wait_send()
    for rnd in range(ROUNDS):
        right_copy(rnd).wait_send()
        for w in range(2):
            sum_copy(rnd, w).wait_send()

    def sent(i, carry):
        spread_copy(0, i).wait_send()
        return carry

    lax.fori_loop(0, RING * SIDES - 1, sent, 0)

    def last(i, carry):
        spread_copy(1, i).wait()
        return carry

    lax.fori_loop(0, RING * SIDES, last, 0)
    result = result + jnp.sum(incoming[1].astype(jnp.float32), axis=0)
    bands = out.shape[1]
    for w in range(2):
        out[w] = result[w * bands : (w + 1) * bands] * (1.0 / math.sqrt(grid_count))


def per_device(pairs, screening, kq_index, umklapp, occupancy):
    rounds, k_count, band_count, summed_count, column_count = pairs.shape
    rows = band_count * summed_count
    grid_count = screening.shape[2]
    devices = grid_count // column_count
    bands = band_count // devices
    chips = RING * SIDES
    sigma = pl.pallas_call(
        kernel,
        out_shape=jax.ShapeDtypeStruct((2, bands, band_count), jnp.float32),
        in_specs=[
            pl.BlockSpec(memory_space=pl.ANY),
            pl.BlockSpec(memory_space=pl.ANY),
            pl.BlockSpec(memory_space=pl.ANY),
            pl.BlockSpec(memory_space=pl.ANY),
            pl.BlockSpec(memory_space=pl.ANY),
        ],
        out_specs=pl.BlockSpec(memory_space=pltpu.VMEM),
        scratch_shapes=[
            pltpu.VMEM((chips, rows, column_count), jnp.bfloat16),
            pltpu.VMEM((chips, rows, column_count), jnp.bfloat16),
            pltpu.VMEM((CORES, 2, devices + 1, LANES, column_count), jnp.bfloat16),
            pltpu.VMEM((ROUNDS, LANES, 2 * LANES), jnp.bfloat16),
            pltpu.VMEM((ROUNDS, 2 * CORES, rows, column_count), jnp.float32),
            pltpu.VMEM((CORES, rows, column_count), jnp.float32),
            pltpu.VMEM((ROUNDS, CORES, rows, column_count), jnp.bfloat16),
            pltpu.VMEM((ROUNDS, CORES, rows, column_count), jnp.bfloat16),
            pltpu.VMEM((ROUNDS, 2, chips, 2, bands, band_count), jnp.float32),
            pltpu.VMEM((ROUNDS, 2, chips, bands, band_count), jnp.float32),
            pltpu.VMEM((ROUNDS, chips, 2 * bands, band_count), jnp.bfloat16),
            pltpu.VMEM((ROUNDS, chips, 2 * bands, band_count), jnp.bfloat16),
            pltpu.VMEM((3, LANES, 2 * CORES * column_count), jnp.bfloat16),
            pltpu.SMEM(kq_index.shape, jnp.int32),
            pltpu.SMEM(umklapp.shape, jnp.int32),
            pltpu.SMEM(occupancy.shape[::-1], jnp.float32),
            pltpu.SemaphoreType.DMA((COUNT,)),
            pltpu.SemaphoreType.DMA((COUNT,)),
            pltpu.SemaphoreType.DMA((6,)),
        ],
        compiler_params=pltpu.CompilerParams(
            collective_id=0, has_side_effects=True, vmem_limit_bytes=62 << 20
        ),
    )(
        pairs.reshape(rounds, rows, column_count),
        screening.reshape(2, devices, LANES, column_count),
        kq_index,
        umklapp,
        occupancy.T,
    )
    return sigma[None]


def solution(mesh):
    return jax.shard_map(
        per_device,
        mesh=mesh,
        in_specs=(P(None, "kgrp", None, None, "ga"), P("kgrp", None, None, "ga"), P(), P(), P()),
        out_specs=P("kgrp", None, "ga", None),
        check_vma=False,
    )
```

time: 65 us -> 62.8 us (0.966)
  Pallas kernels: 63.4 us -> 61.3 us
    pallas_call x1, Pallas kernels: 63.4 us -> 61.3 us  [per_device(): pl.pallas_call(kernel, out_shape=jax.ShapeDtypeStruct((2, bands, band_cou...]
where the time goes in v3:
time: 62.8 us; the launch traced here: 62.6 us
  Pallas kernels  61.3 us (98%)
  local copies, waits for them, and re-layouts  1.32 us (2%)
    pallas_call x1, Pallas kernels, per_device(): pl.pallas_call(kernel, out_shape=jax.ShapeDtypeStruct((2, bands, band_cou...  61.3 us
    unnamed x1, local copies, waits for them, and re-layouts  1.32 us

profile of v3, /device:TPU:1, one launch (start us, length us, event | category | flops | bytes accessed | tf_op | source)
XLA Modules:
  0.0 62.6 jit_solution(8091959488927757030)
XLA Ops:
  0.0 61.3 %shard_map.55 = f32[2,8,256]{2,1,0:T(8,128)} custom-call(bf16[2,512,128]{2,1,0:T(8,128)(2,1)} %bitcast.5, bf16[2,32,128,128]{3,2,1,0:T(8,128)(2,1)} %bitcast.4, s32[2,16]{1,0:T(2,128)} %kq_index_all.1, s32[2,16]{1,0:T(2,128)} %umklapp_all.1, f32[2,16]{1,0:T(2,128)} %bitcast.7), custom_call_target="tpu_custom_call" | custom-call | tf_op jit(solution)/shard_map/pallas_call | solution.py:419
  61.3 1.3 %copy.7 = f32[1,2,8,256]{3,2,1,0:T(8,128)} copy(f32[1,2,8,256]{3,2,1,0:T(8,128)} %bitcast.6) | data formatting | bytes 32768

commit v4 on v3

--- a/solution.py
+++ b/solution.py
@@ -169,7 +169,6 @@
         across,
         sibling,
         (after, place),
-        (before, place),
     ):
         pl.semaphore_signal(barrier, inc=1, device_id=device, device_id_type=MESH)
     whole = pltpu.make_async_copy(screening, screen.at[core, :, pl.ds(0, tiles)], local.at[0])
@@ -186,7 +185,7 @@
     ]
     for table in tables:
         table.start()
-    pl.semaphore_wait(barrier, 6)
+    pl.semaphore_wait(barrier, 5)
 
     for part in range(PARTS):
         ring_copy(0, 0, 0, 1, part).start()
@@ -360,9 +359,10 @@
     contract(0)
     take_ring(1, 1, 3)
     spread(0)
+    multiply(1, (1, 5), (1, 6), met=jnp.concatenate([last_rows[i] for i in range(2)], axis=0))
     take_across(1, 7)
     swap_right(1)
-    multiply(1, (1, 5), (1, 6), (1, 7), met=jnp.concatenate([last_rows[i] for i in range(3)], axis=0))
+    multiply(1, (1, 7), met=last_rows[2])
     contract(1)
     spread(1)
 

time: 62.8 us -> 62.8 us (level)
  no operation moved by 1% of the time
where the time goes in v4:
time: 62.8 us; the launch traced here: 62.6 us
  Pallas kernels  61.3 us (98%)
  local copies, waits for them, and re-layouts  1.32 us (2%)
    pallas_call x1, Pallas kernels, per_device(): pl.pallas_call(kernel, out_shape=jax.ShapeDtypeStruct((2, bands, band_cou...  61.3 us
    unnamed x1, local copies, waits for them, and re-layouts  1.32 us

profile of v4, /device:TPU:1, one launch (start us, length us, event | category | flops | bytes accessed | tf_op | source)
XLA Modules:
  0.0 62.6 jit_solution(13782442726129970114)
XLA Ops:
  0.0 61.3 %shard_map.55 = f32[2,8,256]{2,1,0:T(8,128)} custom-call(bf16[2,512,128]{2,1,0:T(8,128)(2,1)} %bitcast.5, bf16[2,32,128,128]{3,2,1,0:T(8,128)(2,1)} %bitcast.4, s32[2,16]{1,0:T(2,128)} %kq_index_all.1, s32[2,16]{1,0:T(2,128)} %umklapp_all.1, f32[2,16]{1,0:T(2,128)} %bitcast.7), custom_call_target="tpu_custom_call" | custom-call | tf_op jit(solution)/shard_map/pallas_call | solution.py:419
  61.3 1.3 %copy.7 = f32[1,2,8,256]{3,2,1,0:T(8,128)} copy(f32[1,2,8,256]{3,2,1,0:T(8,128)} %bitcast.6) | data formatting | bytes 32768

commit v5 on v4

--- a/solution.py
+++ b/solution.py
@@ -192,8 +192,6 @@
         ring_copy(0, 0, 1, 1, part).start()
         cross_copy(0, 0, part, own=True).start()
         group_copy(part).start()
-    for again in range(2):
-        screen_copy(again).start()
     for table in tables:
         table.wait()
 
@@ -315,6 +313,8 @@
         lax.fori_loop(0, RING * SIDES - 1 + rnd, one, 0)
 
     take_ring(0, 0, 1, hand_across=False)
+    for again in range(2):
+        screen_copy(again).start()
     take_group()
     for part in range(PARTS):
         for k in (1, 2):

time: 62.8 us -> 62.3 us (level)
  no operation moved by 1% of the time
where the time goes in v5:
time: 62.3 us; the launch traced here: 62.1 us
  Pallas kernels  60.7 us (97%)
  local copies, waits for them, and re-layouts  1.32 us (2%)
    pallas_call x1, Pallas kernels, per_device(): pl.pallas_call(kernel, out_shape=jax.ShapeDtypeStruct((2, bands, band_cou...  60.7 us
    unnamed x1, local copies, waits for them, and re-layouts  1.32 us

profile of v5, /device:TPU:1, one launch (start us, length us, event | category | flops | bytes accessed | tf_op | source)
XLA Modules:
  0.0 62.1 jit_solution(6933620155193342789)
XLA Ops:
  0.0 60.7 %shard_map.55 = f32[2,8,256]{2,1,0:T(8,128)} custom-call(bf16[2,512,128]{2,1,0:T(8,128)(2,1)} %bitcast.5, bf16[2,32,128,128]{3,2,1,0:T(8,128)(2,1)} %bitcast.4, s32[2,16]{1,0:T(2,128)} %kq_index_all.1, s32[2,16]{1,0:T(2,128)} %umklapp_all.1, f32[2,16]{1,0:T(2,128)} %bitcast.7), custom_call_target="tpu_custom_call" | custom-call | tf_op jit(solution)/shard_map/pallas_call | solution.py:419
  60.7 1.3 %copy.7 = f32[1,2,8,256]{3,2,1,0:T(8,128)} copy(f32[1,2,8,256]{3,2,1,0:T(8,128)} %bitcast.6) | data formatting | bytes 32768
